TPU v7x, 32 devices: a whole 2x2x4 slice. The times are simulated.
32 devices in a mesh: dp: 8 (over z, x), tensor: 4 (over y, core).
Axes of the slice: x: 2, y: 2, z: 4, core: 2. Of those that a mesh axis runs over, the one named last changes fastest.
Arguments:
- tokens: bfloat16 [32768, 768], P(('dp', 'tensor')), may hold values from -6 to 6
- bucket: int32 [8], P('dp'), may hold values from 0 to 2, as said below
- lengths: int32 [8, 32], P('dp'), may hold values from 0 to 512, as said below
- w_query: bfloat16 [768, 768], P(None, 'tensor'), may hold values from -0.21875 to 0.21875
- b_query: bfloat16 [768], P('tensor'), may hold values from -1.75 to 1.75
- w_key: bfloat16 [768, 768], P(None, 'tensor'), may hold values from -0.21875 to 0.21875
- w_value: bfloat16 [768, 768], P(None, 'tensor'), may hold values from -0.21875 to 0.21875
- b_value: bfloat16 [768], P('tensor'), may hold values from -1.75 to 1.75
- w_out: bfloat16 [768, 768], P('tensor'), may hold values from -0.875 to 0.875
- b_out: bfloat16 [768], replicated, may hold values from -1.75 to 1.75
- norm1_gain: float32 [768], replicated, may hold values from 0.1 to 1.9
- norm1_shift: float32 [768], replicated, may hold values from -1.75 to 1.75
- w_in: bfloat16 [768, 3072], P(None, 'tensor'), may hold values from -0.21875 to 0.21875
- b_in: bfloat16 [3072], P('tensor'), may hold values from -3 to 3
- w_down: bfloat16 [3072, 768], P('tensor'), may hold values from -0.109375 to 0.109375
- b_down: bfloat16 [768], replicated, may hold values from -1.75 to 1.75
- norm2_gain: float32 [768], replicated, may hold values from 0.1 to 1.9
- norm2_shift: float32 [768], replicated, may hold values from -1.75 to 1.75
- cotangent: float32 [32768, 768], P(('dp', 'tensor')), may hold values from -6 to 6
Outputs:
- block_out: bfloat16 [32768, 768], P(('dp', 'tensor'))
- grad_tokens: float32 [32768, 768], P(('dp', 'tensor'))
- grad_w_query: float32 [768, 768], P(None, 'tensor')
- grad_b_query: float32 [768], P('tensor')
- grad_w_key: float32 [768, 768], P(None, 'tensor')
- grad_w_value: float32 [768, 768], P(None, 'tensor')
- grad_b_value: float32 [768], P('tensor')
- grad_w_out: float32 [768, 768], P('tensor')
- grad_b_out: float32 [768], replicated
- grad_norm1_gain: float32 [768], replicated
- grad_norm1_shift: float32 [768], replicated
- grad_w_in: float32 [768, 3072], P(None, 'tensor')
- grad_b_in: float32 [3072], P('tensor')
- grad_w_down: float32 [3072, 768], P('tensor')
- grad_b_down: float32 [768], replicated
- grad_norm2_gain: float32 [768], replicated
- grad_norm2_shift: float32 [768], replicated
Inputs may be any that keep to these rules, and one draw needn't show every extreme that they name: bucket[g] sets the row length of group g (128, 256, 512); group 0 has bucket 2 and group 1 bucket 0. `lengths`: for group g with row length L, entries 0 to 4096/L - 1 are 1 to L, entry 0 equal to L; later entries are 0.
All inputs are finite; a program needn't handle non-finite values.
Results may differ from a plain program's by a relative error of at most 0.015.
The roundings to bfloat16 on the way count: a program that leaves them out, or rounds other values in their place, can miss the bound.
Values may be sent and summed in bfloat16 or wider, within the bound.
No kernel may reach another device: no remote copies, remote signals or barrier semaphores. Data moves between devices by JAX's collectives and lax.ppermute only.
A program may use at most 192 MiB of HBM per device.

v0:
```python
import jax
import jax.numpy as jnp
from jax import lax
from jax.sharding import PartitionSpec as P

HEAD = 64
BLOCK = 512


EPSILON = 1e-12


def norm_rows(values, gain, shift):
    mean = jnp.mean(values, axis=-1, keepdims=True)
    centred = values - mean
    spread = jnp.mean(centred * centred, axis=-1, keepdims=True)
    return centred * lax.rsqrt(spread + EPSILON) * gain + shift


def exact_gelu(values):
    return jax.nn.gelu(values, approximate=False)


def rows_product(left, right):
    return lax.dot_general(
        left, right, (((0,), (0,)), ((), ())), preferred_element_type=jnp.float32
    )


def back_product(left, right):
    return lax.dot_general(
        left, right, (((1,), (1,)), ((), ())), preferred_element_type=jnp.float32
    )


def row_layout(bucket, lengths, token_count):
    bucket_kind = bucket[0]
    row_len = jnp.where(
        bucket_kind == 0, BLOCK // 4, jnp.where(bucket_kind == 1, BLOCK // 2, BLOCK)
    )
    places = jnp.arange(token_count, dtype=jnp.int32)
    row_of = places // row_len
    inside = places % row_len
    length_table = lengths[0]
    picked = row_of[:, None] == jnp.arange(length_table.shape[0], dtype=jnp.int32)[None, :]
    length_of = jnp.sum(jnp.where(picked, length_table[None, :], 0), axis=1)
    return (row_of, inside < length_of)


def masked_scores(query_blk, key_blk, row_blk, valid_blk):
    scores = jnp.einsum(
        "qhd,khd->hqk", query_blk, key_blk, preferred_element_type=jnp.float32
    ) * HEAD ** (-0.5)
    allowed = (row_blk[:, None] == row_blk[None, :]) & valid_blk[None, :]
    return jnp.where(allowed[None], scores, -1000000000.0)


def blocked(values, head_count):
    return values.reshape(values.shape[0] // BLOCK, BLOCK, head_count, HEAD)


def attend_forward(queries, key_rows, vals, row_of, valid):
    head_count = queries.shape[1] // HEAD
    token_count = queries.shape[0]

    def one_block(block_items):
        query_blk, key_blk, value_blk, row_blk, valid_blk = block_items
        scores = masked_scores(query_blk, key_blk, row_blk, valid_blk)
        largest = jnp.max(scores, axis=-1, keepdims=True)
        raised = jnp.exp(scores - largest)
        row_total = jnp.sum(raised, axis=-1, keepdims=True)
        probs = (raised / row_total).astype(jnp.bfloat16)
        context = jnp.einsum("hqk,khd->qhd", probs, value_blk, preferred_element_type=jnp.float32)
        return (context, (largest + jnp.log(row_total))[..., 0])

    context, log_total = lax.map(
        one_block,
        (
            blocked(queries, head_count),
            blocked(key_rows, head_count),
            blocked(vals, head_count),
            row_of.reshape(-1, BLOCK),
            valid.reshape(-1, BLOCK),
        ),
    )
    return (context.reshape(token_count, head_count * HEAD), log_total)


def attend_backward(queries, key_rows, vals, grad_context, log_total, row_of, valid):
    head_count = queries.shape[1] // HEAD
    token_count = queries.shape[0]

    def one_block(block_items):
        query_blk, key_blk, value_blk, grad_blk, log_blk, row_blk, valid_blk = block_items
        scores = masked_scores(query_blk, key_blk, row_blk, valid_blk)
        probs = jnp.exp(scores - log_blk[..., None])
        grad_probs = jnp.einsum(
            "qhd,khd->hqk", grad_blk, value_blk, preferred_element_type=jnp.float32
        )
        centre = jnp.sum(probs * grad_probs, axis=-1, keepdims=True)
        grad_scores = (probs * (grad_probs - centre)).astype(jnp.bfloat16)
        grad_queries = jnp.einsum(
            "hqk,khd->qhd", grad_scores, key_blk, preferred_element_type=jnp.float32
        ) * HEAD ** (-0.5)
        grad_keys = jnp.einsum(
            "hqk,qhd->khd", grad_scores, query_blk, preferred_element_type=jnp.float32
        ) * HEAD ** (-0.5)
        grad_vals = jnp.einsum(
            "hqk,qhd->khd", probs.astype(jnp.bfloat16), grad_blk, preferred_element_type=jnp.float32
        )
        return (grad_queries, grad_keys, grad_vals)

    grad_queries, grad_keys, grad_vals = lax.map(
        one_block,
        (
            blocked(queries, head_count),
            blocked(key_rows, head_count),
            blocked(vals, head_count),
            blocked(grad_context, head_count),
            log_total,
            row_of.reshape(-1, BLOCK),
            valid.reshape(-1, BLOCK),
        ),
    )
    full_shape = (token_count, head_count * HEAD)
    return (
        grad_queries.reshape(full_shape),
        grad_keys.reshape(full_shape),
        grad_vals.reshape(full_shape),
    )


def run_layer(token_shard, cot_shard, weights, smalls, row_of, valid, hooks):
    w_query, w_key, w_value, w_out, w_in, w_down, b_query, b_value, b_in = weights
    b_out, gain1, shift1, b_down, gain2, shift2 = smalls
    (
        tokens_wide,
        attn_total,
        normed_wide,
        ffn_total,
        back_wide,
        back_total,
        resid_wide,
        input_total,
    ) = hooks
    head_width = w_query.shape[1]
    tokens_all = tokens_wide(token_shard)
    w_joined = jnp.concatenate((w_query, w_key, w_value), axis=1)
    b_joined = jnp.concatenate((b_query, jnp.zeros_like(b_query), b_value)).astype(jnp.float32)
    projected = (
        jnp.dot(tokens_all, w_joined, preferred_element_type=jnp.float32) + b_joined
    ).astype(jnp.bfloat16)
    queries = projected[:, :head_width]
    key_rows = projected[:, head_width : 2 * head_width]
    vals = projected[:, 2 * head_width :]
    context, log_total = attend_forward(queries, key_rows, vals, row_of, valid)
    context = context.astype(jnp.bfloat16)
    attention = attn_total(
        jnp.dot(context, w_out, preferred_element_type=jnp.float32)
    ) + b_out.astype(jnp.float32)
    residual = token_shard.astype(jnp.float32) + attention
    normed = norm_rows(residual, gain1, shift1)
    normed_all = normed_wide(normed.astype(jnp.bfloat16))
    pre_act = jnp.dot(normed_all, w_in, preferred_element_type=jnp.float32) + b_in.astype(
        jnp.float32
    )
    activated = exact_gelu(pre_act).astype(jnp.bfloat16)
    ffn_out = ffn_total(
        jnp.dot(activated, w_down, preferred_element_type=jnp.float32)
    ) + b_down.astype(jnp.float32)
    summed = normed + ffn_out
    result, norm2_pull = jax.vjp(norm_rows, summed, gain2, shift2)
    grad_summed, grad_gain2, grad_shift2 = norm2_pull(cot_shard)
    grad_ffn = grad_summed.astype(jnp.bfloat16)
    grad_bdown = jnp.sum(grad_ffn.astype(jnp.float32), axis=0)
    grad_ffn_all = back_wide(grad_ffn)
    grad_wdown = rows_product(activated, grad_ffn_all)
    grad_act = back_product(grad_ffn_all, w_down)
    grad_pre = jax.vjp(exact_gelu, pre_act)[1](grad_act)[0].astype(jnp.bfloat16)
    grad_win = rows_product(normed_all, grad_pre)
    grad_bin = jnp.sum(grad_pre.astype(jnp.float32), axis=0)
    grad_normed = grad_summed + back_total(back_product(grad_pre, w_in))
    grad_resid, grad_gain1, grad_shift1 = jax.vjp(norm_rows, residual, gain1, shift1)[1](
        grad_normed
    )
    grad_attn = grad_resid.astype(jnp.bfloat16)
    grad_bout = jnp.sum(grad_attn.astype(jnp.float32), axis=0)
    grad_attn_all = resid_wide(grad_attn)
    grad_wout = rows_product(context, grad_attn_all)
    grad_context = back_product(grad_attn_all, w_out).astype(jnp.bfloat16)
    grad_queries, grad_keys, grad_vals = attend_backward(
        queries, key_rows, vals, grad_context, log_total, row_of, valid
    )
    grad_joined = jnp.concatenate((grad_queries, grad_keys, grad_vals), axis=1).astype(jnp.bfloat16)
    grad_wjoined = rows_product(tokens_all, grad_joined)
    grad_bjoined = jnp.sum(grad_joined.astype(jnp.float32), axis=0)
    grad_input = grad_resid + input_total(back_product(grad_joined, w_joined))
    split_grads = (
        grad_wjoined[:, :head_width],
        grad_wjoined[:, head_width : 2 * head_width],
        grad_wjoined[:, 2 * head_width :],
        grad_wout,
        grad_win,
        grad_wdown,
        grad_bjoined[:head_width],
        grad_bjoined[2 * head_width :],
        grad_bin,
    )
    small_grads = (grad_bout, grad_gain1, grad_shift1, grad_bdown, grad_gain2, grad_shift2)
    return (split_grads, small_grads, result.astype(jnp.bfloat16), grad_input)


def per_device(
    tokens,
    bucket,
    lengths,
    w_query,
    b_query,
    w_key,
    w_value,
    b_value,
    w_out,
    b_out,
    norm1_gain,
    norm1_shift,
    w_in,
    b_in,
    w_down,
    b_down,
    norm2_gain,
    norm2_shift,
    cotangent,
):
    shard_rows = tokens.shape[0]
    smalls = (b_out, norm1_gain, norm1_shift, b_down, norm2_gain, norm2_shift)
    weights = (w_query, w_key, w_value, w_out, w_in, w_down, b_query, b_value, b_in)
    row_of, valid = row_layout(bucket, lengths, shard_rows * lax.axis_size("tensor"))

    def tokens_wide(values):
        return lax.all_gather(values, "tensor", axis=0, tiled=True)

    def attn_total(values):
        return lax.psum_scatter(values, "tensor", scatter_dimension=0, tiled=True)

    def normed_wide(values):
        return lax.all_gather(values, "tensor", axis=0, tiled=True)

    def ffn_total(values):
        return lax.psum_scatter(values, "tensor", scatter_dimension=0, tiled=True)

    def back_wide(values):
        return lax.all_gather(values, "tensor", axis=0, tiled=True)

    def back_total(values):
        return lax.psum_scatter(values, "tensor", scatter_dimension=0, tiled=True)

    def resid_wide(values):
        return lax.all_gather(values, "tensor", axis=0, tiled=True)

    def input_total(values):
        return lax.psum_scatter(
            values.astype(jnp.bfloat16), "tensor", scatter_dimension=0, tiled=True
        ).astype(jnp.float32)

    hooks = (
        tokens_wide,
        attn_total,
        normed_wide,
        ffn_total,
        back_wide,
        back_total,
        resid_wide,
        input_total,
    )
    split_grads, small_grads, block_out, grad_tokens = run_layer(
        tokens, cotangent, weights, smalls, row_of, valid, hooks
    )
    split_grads = lax.psum(
        (
            split_grads[0],
            split_grads[1],
            split_grads[2],
            split_grads[3],
            split_grads[4],
            split_grads[5],
            split_grads[6],
            split_grads[7],
            split_grads[8],
        ),
        "dp",
    )
    small_grads = lax.psum(
        (
            small_grads[0],
            small_grads[1],
            small_grads[2],
            small_grads[3],
            small_grads[4],
            small_grads[5],
        ),
        ("dp", "tensor"),
    )
    grad_wq, grad_wk, grad_wv, grad_wo, grad_wi, grad_wd, grad_bq, grad_bv, grad_bi = split_grads
    grad_bo, grad_g1, grad_s1, grad_bd, grad_g2, grad_s2 = small_grads
    return (
        block_out,
        grad_tokens,
        grad_wq,
        grad_bq,
        grad_wk,
        grad_wv,
        grad_bv,
        grad_wo,
        grad_bo,
        grad_g1,
        grad_s1,
        grad_wi,
        grad_bi,
        grad_wd,
        grad_bd,
        grad_g2,
        grad_s2,
    )


def solution(mesh):
    in_specs = (
        P(("dp", "tensor"), None),
        P("dp"),
        P("dp", None),
        P(None, "tensor"),
        P("tensor"),
        P(None, "tensor"),
        P(None, "tensor"),
        P("tensor"),
        P("tensor", None),
        P(),
        P(),
        P(),
        P(None, "tensor"),
        P("tensor"),
        P("tensor", None),
        P(),
        P(),
        P(),
        P(("dp", "tensor"), None),
    )
    out_specs = (
        P(("dp", "tensor"), None),
        P(("dp", "tensor"), None),
        P(None, "tensor"),
        P("tensor"),
        P(None, "tensor"),
        P(None, "tensor"),
        P("tensor"),
        P("tensor", None),
        P(),
        P(),
        P(),
        P(None, "tensor"),
        P("tensor"),
        P("tensor", None),
        P(),
        P(),
        P(),
    )
    return jax.shard_map(
        per_device, mesh=mesh, in_specs=in_specs, out_specs=out_specs, check_vma=False
    )
```

profile of v0, /device:TPU:0, one launch (start us, length us, event | category | flops | bytes accessed | tf_op | source)
XLA Modules:
  0.0 1113.3 jit_solution(5481374400176954208)
XLA Ops:
  13.9 44.8 %all-gather.5.cloned.1.call-done = bf16[4096,768]{1,0:T(8,128)(2,1)} async-done(((bf16[1024,768]{1,0:T(8,128)(2,1)}), bf16[4096,768]{1,0:T(8,128)(2,1)}) %all-gather.5.cloned.1.call-update) | async-done | bytes 6291472 | tf_op jit(solution)/shard_map/all_gather | solution.py:240
  58.7 6.9 fusion.54
  73.0 47.8 %while.26 = (s32[]{:T(128)}, bf16[8,512,3,64]{1,3,2,0:T(8,128)(2,1)}, f32[8,3,512]{2,1,0:T(4,128)}, bf16[8,512,3,64]{1,3,2,0:T(8,128)(2,1)}, s32[8,512]{1,0:T(8,...) while((s32[]{:T(128)}, ...), condition=%wide.region_4.5_spmd, body=%wide.region_1.4_spmd.sunk | while | flops 211286528 | bytes 11530341 | solution.py:76
  125.6 6.4 fusion.73
  132.7 98.5 %reduce-scatter.5.cloned.1.call-done = f32[1024,768]{1,0:T(8,128)} async-done(((f32[4096,768]{1,0:T(8,128)}), f32[1024,768]{1,0:T(8,128)}) %reduce-scatter.5.cloned.1.call-update) | async-done | bytes 3145744 | tf_op jit(solution)/shard_map/reduce_scatter | solution.py:243
  237.1 46.5 %all-gather.7.cloned.1.call-done = bf16[4096,768]{1,0:T(8,128)(2,1)} async-done(((bf16[1024,768]{1,0:T(8,128)(2,1)}), bf16[4096,768]{1,0:T(8,128)(2,1)}) %all-gather.7.cloned.1.call-update) | async-done | bytes 6291472 | tf_op jit(solution)/shard_map/all_gather | solution.py:246
  283.6 34.0 %multiply_convert_fusion.1 = (bf16[4096,768]{1,0:T(8,128)(2,1)S(1)}, f32[4096,768]{1,0:T(8,128)}, f32[4096,768]{1,0:T(8,128)}) fusion(f32[768]{0:T(1024)S(1)} %convert_element_type.88, bf16[4096,768]{1,0:T(8,128)(2,1)} %all-gather.7.cloned.1.call-done, bf16[768,768]{1,0:T(8,128)(2,1)S(1)} %copy-done), kind=kOutput, calls=%fused_computation.64 | convolution fusion | flops 5039456256 | bytes 38931456 | tf_op jit(solution)/shard_map/dot_general | solution.py:164
  320.2 8.1 fusion.74
  329.0 98.6 %reduce-scatter.7.cloned.1.call-done = f32[1024,768]{1,0:T(8,128)} async-done(((f32[4096,768]{1,0:T(8,128)}), f32[1024,768]{1,0:T(8,128)}) %reduce-scatter.7.cloned.1.call-update) | async-done | bytes 3145744 | tf_op jit(solution)/shard_map/reduce_scatter | solution.py:249
  440.9 46.3 %all-gather.9.cloned.1.call-done = bf16[4096,768]{1,0:T(8,128)(2,1)} async-done(((bf16[1024,768]{1,0:T(8,128)(2,1)}), bf16[4096,768]{1,0:T(8,128)(2,1)}) %all-gather.9.cloned.1.call-update) | async-done | bytes 6291472 | tf_op jit(solution)/shard_map/all_gather | solution.py:252
  487.2 17.5 %convert_reduce_fusion = (f32[768]{0:T(1024)S(1)}, bf16[4096,768]{1,0:T(8,128)(2,1)}) fusion(f32[4096,768]{1,0:T(8,128)} %get-tuple-element.254, f32[4096,768]{1,0:T(8,128)} %get-tuple-element.270, f32[768]{0:T(1024)S(1)} %convert_element_type.88, bf16[4096,768]{1,0:T(8,128)(2,1)} %all-gather.9.cloned.1.call-done, bf16[768,768]{1,0:T(8,128)(2,1)S(1)} %copy-done.31), kind=kOutput, calls=%fused_computation.62 | convolution fusion | flops 4885314560 | bytes 38934528 | tf_op jit(solution)/shard_map/dot_general | solution.py:31
  504.7 10.6 fusion.75
  515.4 99.2 %reduce-scatter.9.cloned.1.call-done = f32[1024,768]{1,0:T(8,128)} async-done(((f32[4096,768]{1,0:T(8,128)}), f32[1024,768]{1,0:T(8,128)}) %reduce-scatter.9.cloned.1.call-update) | async-done | bytes 3145744 | tf_op jit(solution)/shard_map/reduce_scatter | solution.py:255
  614.5 4.8 multiply_reduce_fusion.2
  624.0 46.5 %all-gather.11.cloned.1.call-done = bf16[4096,768]{1,0:T(8,128)(2,1)} async-done(((bf16[1024,768]{1,0:T(8,128)(2,1)}), bf16[4096,768]{1,0:T(8,128)(2,1)}) %all-gather.11.cloned.1.call-update) | async-done | bytes 6291472 | tf_op jit(solution)/shard_map/all_gather | solution.py:258
  670.5 5.0 convolution_convert_fusion.1
  680.6 94.3 %while.27 = (s32[]{:T(128)}, bf16[8,512,3,64]{1,3,2,0:T(8,128)(2,1)}, bf16[8,512,3,64]{1,3,2,0:T(8,128)(2,1)}, bf16[8,512,3,64]{1,3,2,0:T(8,128)(2,1)}, bf16[8,5...) while((s32[]{:T(128)}, ...), condition=%wide.region_18.19_spmd, body=%wide.region_16.18_spmd.sunk | while | flops 511113728 | bytes 26716800 | solution.py:113
  785.4 7.0 convolution_convert_fusion
  792.5 10.4 fusion.78
  802.9 10.7 fusion.77
  821.8 40.7 %all-reduce = (f32[768]{0:T(1024)}, f32[768]{0:T(1024)}, f32[768]{0:T(1024)}, f32[768]{0:T(1024)}, f32[768]{0:T(1024)}, /*index=5*/f32[768]{0:T(1024)}) all-reduce(f32[768]{0:T(1024)S(1)} %get-tuple-element.242, f32[768]{0:T(1024)S(1)} %get-tuple-element.183, ...), channel_id=1, replica_groups=mesh['dp'=8,'tensor'=4] {'dp','tensor'}, use_global_device_ids=true, to_apply=%region_28.29 | all-reduce | flops 4608 | bytes 36864 | tf_op jit(solution)/shard_map/psum | solution.py:292
  866.3 22.5 %all-reduce.1 = (f32[192]{0:T(256)}, f32[192]{0:T(256)}, f32[768]{0:T(1024)}) all-reduce(f32[192]{0:T(256)S(1)} %get-tuple-element.269, f32[192]{0:T(256)S(1)} %get-tuple-element.268, f32[768]{0:T(1024)S(1)} %get-tuple-element.244), channel_id=1, replica_groups=mesh['dp'=8,'tensor'=4] {'dp'}, use_global_device_ids=true, to_apply=%region_22.23 | all-reduce | flops 1152 | bytes 9216 | tf_op jit(solution)/shard_map/psum | solution.py:278
  888.8 4.4 convert_add_fusion
  893.2 203.6 %all-reduce.5.cloned.1.call-done = (f32[768,192]{0,1:T(8,128)}, f32[768,192]{0,1:T(8,128)}, f32[768,192]{0,1:T(8,128)}, f32[192,768]{1,0:T(8,128)}, f32[768,768]{1,0:T(8,128)}, /*index=5*/f32[768,768]{1,0:T(8,128)}) async-done(((f32[768,192]{0,1:T(8,128)}, f32[768,192]{0,1:T(8,128)}, f32[768,192]{0,1:T(8,128)}, f32[192,768]{1,0:T(8,128)}, f32[768,768]{1,0:T(8,128)}, /*index=5*/f32[768,768]{1,0:T(8,128)}), ...) | async-done | bytes 7077904 | tf_op jit(solution)/shard_map/psum | solution.py:278
  (303 shorter events, 224.2 us)
Async XLA Ops:
  7.2 276.4 %copy-start = (bf16[768,768]{1,0:T(8,128)(2,1)S(1)}, bf16[768,768]{1,0:T(8,128)(2,1)}, u32[]{:S(2)}) copy-start(bf16[768,768]{1,0:T(8,128)(2,1)} %param.35) | copy-start | bytes 3538948
  7.2 51.5 %all-gather.5.cloned.1.call-start = ((), (), s32[]{:S(2)}) async-start(), calls=%async_computation.4 | async-start | bytes 7864320 | tf_op jit(solution)/shard_map/all_gather | solution.py:240
  7.9 223.3 %reduce-scatter.5.cloned.1.call-start = ((), (), s32[]{:S(2)}) async-start(), calls=%async_computation.5 | async-start | bytes 15728640 | tf_op jit(solution)/shard_map/reduce_scatter | solution.py:243
  13.6 52.0 %copy-start.19 = (bf16[768,576]{0,1:T(8,128)(2,1)}, bf16[768,576]{0,1:T(8,128)(2,1)S(1)}, u32[]{:S(2)}) copy-start(bf16[768,576]{0,1:T(8,128)(2,1)S(1)} %constant_dynamic-update-slice_fusion) | copy-start | bytes 2654212
  132.1 99.2 %copy-start.11 = (bf16[1024,768]{1,0:T(8,128)(2,1)S(1)}, bf16[1024,768]{1,0:T(8,128)(2,1)}, u32[]{:S(2)}) copy-start(bf16[1024,768]{1,0:T(8,128)(2,1)} %param.23) | copy-start | bytes 4718596
  132.1 151.5 %all-gather.7.cloned.1.call-start = ((), (), s32[]{:S(2)}) async-start(), calls=%async_computation.6 | async-start | bytes 7864320 | tf_op jit(solution)/shard_map/all_gather | solution.py:246
  237.1 190.5 %reduce-scatter.7.cloned.1.call-start = ((), (), s32[]{:S(2)}) async-start(), calls=%async_computation.7 | async-start | bytes 15728640 | tf_op jit(solution)/shard_map/reduce_scatter | solution.py:249
  237.1 83.1 %copy-start.31 = (bf16[768,768]{1,0:T(8,128)(2,1)S(1)}, bf16[768,768]{1,0:T(8,128)(2,1)}, u32[]{:S(2)}) copy-start(bf16[768,768]{1,0:T(8,128)(2,1)} %param.37) | copy-start | bytes 3538948
  328.3 158.9 %all-gather.9.cloned.1.call-start = ((), (), s32[]{:S(2)}) async-start(), calls=%async_computation.8 | async-start | bytes 7864320 | tf_op jit(solution)/shard_map/all_gather | solution.py:252
  440.6 173.9 %reduce-scatter.9.cloned.1.call-start = ((), (), s32[]{:S(2)}) async-start(), calls=%async_computation.9 | async-start | bytes 15728640 | tf_op jit(solution)/shard_map/reduce_scatter | solution.py:255
  515.3 104.0 %copy-start.24 = (f32[1024]{0:T(1024)S(1)}, f32[1024]{0:T(1024)}, u32[]{:S(2)}) copy-start(f32[1024]{0:T(1024)} %copy-done.23) | copy-start | bytes 12292
  515.3 155.2 %all-gather.11.cloned.1.call-start = ((), (), s32[]{:S(2)}) async-start(), calls=%async_computation.10 | async-start | bytes 7864320 | tf_op jit(solution)/shard_map/all_gather | solution.py:258
  614.5 4.8 copy-start.2
  622.5 48.0 %copy-start.16 = (bf16[192,768]{1,0:T(8,128)(2,1)S(1)}, bf16[192,768]{1,0:T(8,128)(2,1)}, u32[]{:S(2)}) copy-start(bf16[192,768]{1,0:T(8,128)(2,1)} %param.31) | copy-start | bytes 884740
  624.0 264.8 %reduce-scatter.11.cloned.1.call-start = ((), (), s32[]{:S(2)}) async-start(), calls=%async_computation.11 | async-start | bytes 7864320 | tf_op jit(solution)/shard_map/reduce_scatter | solution.py:261
  792.4 304.4 %all-reduce.5.cloned.1.call-start = ((), (), s32[]{:S(2)}) async-start(), calls=%async_computation.12 | async-start | bytes 14155776 | tf_op jit(solution)/shard_map/psum | solution.py:278
  792.4 21.2 %slice-start = ((s8[4718592]{0:T(1024)(128)(4,1)}), s8[4194304]{0:T(1024)(128)(4,1)S(1)}, s32[]{:S(2)}) async-start(s8[4718592]{0:T(1024)(128)(4,1)} %bitcast.177), calls=%async_computation.13 | async-start | bytes 8388608
  792.5 21.2 %slice-start.2 = ((s8[6291456]{0:T(1024)(128)(4,1)}), s8[4194304]{0:T(1024)(128)(4,1)S(1)}, s32[]{:S(2)}) async-start(s8[6291456]{0:T(1024)(128)(4,1)} %bitcast.199), calls=%async_computation.15 | async-start | bytes 8388608
  802.9 10.8 slice-start.1
  802.9 10.8 slice-start.3
  802.9 15.9 %slice-start.4 = ((s8[6291456]{0:T(1024)(128)(4,1)}), s8[4194304]{0:T(1024)(128)(4,1)S(1)}, s32[]{:S(2)}) async-start(s8[6291456]{0:T(1024)(128)(4,1)} %bitcast.201), calls=%async_computation.17 | async-start | bytes 8388608
  813.7 5.1 slice-start.5
  1096.8 5.9 copy-start.14
  1096.8 6.7 copy-start.13
  (24 other events, 51.1 us)
Sparse Core Ops, SparseCore 0:
  9.6 49.0 all-gather.4
  132.2 99.0 reduce-scatter.4
  237.2 46.3 all-gather.6
  328.5 99.0 reduce-scatter.6
  440.8 46.3 all-gather.8
  515.4 99.0 reduce-scatter.8
  624.1 46.3 all-gather.10
  792.5 59.0 reduce-scatter.10
  858.6 238.1 all-reduce.4
where the time goes:
time: 1130 us; the launch traced here: 1110 us
  waiting for transfers between devices  685 us (61%)
  matrix products  231 us (20%)
  local copies, waits for them, and re-layouts  63.2 us (6%)
  blocking collectives  63.2 us (6%)
  other arithmetic  53.6 us (5%)
  between operations  15.5 us (1%)
    psum x1, waiting for transfers between devices, per_device(): lax.psum((split_grads[0], split_grads[1], split_grads[2], split_grads[3],...  204 us
    reduce_scatter x1, waiting for transfers between devices, back_total(): return lax.psum_scatter(values, 'tensor', scatter_dimension=0, tiled=True)  99.2 us
    reduce_scatter x1, waiting for transfers between devices, ffn_total(): return lax.psum_scatter(values, 'tensor', scatter_dimension=0, tiled=True)  98.6 us
    reduce_scatter x1, waiting for transfers between devices, attn_total(): return lax.psum_scatter(values, 'tensor', scatter_dimension=0, tiled=True)  98.5 us
    all_gather x1, waiting for transfers between devices, resid_wide(): return lax.all_gather(values, 'tensor', axis=0, tiled=True)  46.5 us
    all_gather x1, waiting for transfers between devices, normed_wide(): return lax.all_gather(values, 'tensor', axis=0, tiled=True)  46.5 us
    all_gather x1, waiting for transfers between devices, back_wide(): return lax.all_gather(values, 'tensor', axis=0, tiled=True)  46.3 us
    all_gather x1, waiting for transfers between devices, tokens_wide(): return lax.all_gather(values, 'tensor', axis=0, tiled=True)  44.8 us
  transfers between devices with their start and end apart: 9, of which 8 were waited for; matrix products, arithmetic and copies ran while one was open for 4% of the time, Pallas kernels for 0%

commit v1 on v0

v1 whole, which is shorter than its diff:
```python
import jax
import jax.numpy as jnp
from jax import lax
from jax.sharding import PartitionSpec as P

HEAD = 64
BLOCK = 512
EPSILON = 1e-12
F32 = jnp.float32
BF16 = jnp.bfloat16


def norm_rows(values, gain, shift):
    mean = jnp.mean(values, axis=-1, keepdims=True)
    centred = values - mean
    spread = jnp.mean(centred * centred, axis=-1, keepdims=True)
    return centred * lax.rsqrt(spread + EPSILON) * gain + shift


def exact_gelu(values):
    return jax.nn.gelu(values, approximate=False)


def product(left, right):
    return jnp.dot(left, right, preferred_element_type=F32)


def rows_product(left, right):
    return lax.dot_general(left, right, (((0,), (0,)), ((), ())), preferred_element_type=F32)


def back_product(left, right):
    return lax.dot_general(left, right, (((1,), (1,)), ((), ())), preferred_element_type=F32)


def row_layout(bucket, lengths, first, token_count):
    bucket_kind = bucket[0]
    row_len = jnp.where(
        bucket_kind == 0, BLOCK // 4, jnp.where(bucket_kind == 1, BLOCK // 2, BLOCK)
    )
    places = first + jnp.arange(token_count, dtype=jnp.int32)
    row_of = places // row_len
    inside = places % row_len
    length_table = lengths[0]
    picked = row_of[:, None] == jnp.arange(length_table.shape[0], dtype=jnp.int32)[None, :]
    length_of = jnp.sum(jnp.where(picked, length_table[None, :], 0), axis=1)
    return (row_of, inside < length_of)


def masked_scores(query_blk, key_blk, row_blk, valid_blk):
    scores = jnp.einsum(
        "qhd,khd->hqk", query_blk, key_blk, preferred_element_type=F32
    ) * HEAD ** (-0.5)
    allowed = (row_blk[:, None] == row_blk[None, :]) & valid_blk[None, :]
    return jnp.where(allowed[None], scores, -1000000000.0)


def blocked(values):
    return values.reshape(values.shape[0] // BLOCK, BLOCK, values.shape[1] // HEAD, HEAD)


def attend_forward(queries, key_rows, vals, row_of, valid):
    def one_block(block_items):
        query_blk, key_blk, value_blk, row_blk, valid_blk = block_items
        scores = masked_scores(query_blk, key_blk, row_blk, valid_blk)
        largest = jnp.max(scores, axis=-1, keepdims=True)
        raised = jnp.exp(scores - largest)
        row_total = jnp.sum(raised, axis=-1, keepdims=True)
        probs = (raised / row_total).astype(BF16)
        context = jnp.einsum("hqk,khd->qhd", probs, value_blk, preferred_element_type=F32)
        return (context, (largest + jnp.log(row_total))[..., 0])

    context, log_total = lax.map(
        one_block,
        (
            blocked(queries),
            blocked(key_rows),
            blocked(vals),
            row_of.reshape(-1, BLOCK),
            valid.reshape(-1, BLOCK),
        ),
    )
    return (context.reshape(queries.shape).astype(BF16), log_total)


def attend_backward(queries, key_rows, vals, grad_context, log_total, row_of, valid):
    def one_block(block_items):
        query_blk, key_blk, value_blk, grad_blk, log_blk, row_blk, valid_blk = block_items
        scores = masked_scores(query_blk, key_blk, row_blk, valid_blk)
        probs = jnp.exp(scores - log_blk[..., None])
        grad_probs = jnp.einsum("qhd,khd->hqk", grad_blk, value_blk, preferred_element_type=F32)
        centre = jnp.sum(probs * grad_probs, axis=-1, keepdims=True)
        grad_scores = (probs * (grad_probs - centre)).astype(BF16)
        grad_queries = jnp.einsum(
            "hqk,khd->qhd", grad_scores, key_blk, preferred_element_type=F32
        ) * HEAD ** (-0.5)
        grad_keys = jnp.einsum(
            "hqk,qhd->khd", grad_scores, query_blk, preferred_element_type=F32
        ) * HEAD ** (-0.5)
        grad_vals = jnp.einsum(
            "hqk,qhd->khd", probs.astype(BF16), grad_blk, preferred_element_type=F32
        )
        return (grad_queries, grad_keys, grad_vals)

    grads = lax.map(
        one_block,
        (
            blocked(queries),
            blocked(key_rows),
            blocked(vals),
            blocked(grad_context),
            log_total,
            row_of.reshape(-1, BLOCK),
            valid.reshape(-1, BLOCK),
        ),
    )
    return tuple(item.reshape(queries.shape).astype(BF16) for item in grads)


def swap(values, axis, bit):
    count = lax.axis_size(axis)
    return lax.ppermute(values, axis, [(at, at ^ bit) for at in range(count)])


def pieces_of(own):
    near = swap(own, "tensor", 1)
    far = swap(own, "tensor", 2)
    return [own, near, far, swap(far, "tensor", 1)]


def dp_bits():
    bits, bit = [], 1
    while bit < lax.axis_size("dp"):
        bits.append(bit)
        bit *= 2
    return bits


def sum_over_dp(values):
    me = lax.axis_index("dp")
    for bit in dp_bits():
        half = values.shape[0] // 2
        mine = (me // bit) % 2
        kept = lax.dynamic_slice_in_dim(values, mine * half, half)
        sent = lax.dynamic_slice_in_dim(values, (1 - mine) * half, half)
        got = swap(sent, "dp", bit)
        values = (kept.astype(F32) + got.astype(F32)).astype(BF16)
    for bit in reversed(dp_bits()):
        mine = (me // bit) % 2
        got = swap(values, "dp", bit)
        values = jnp.where(
            mine == 0, jnp.concatenate((values, got)), jnp.concatenate((got, values))
        )
    return values


def to_owner(parts):
    g0, g1, g2, g3 = [part.astype(BF16) for part in parts]
    far = (g2.astype(F32) + swap(g3, "tensor", 1).astype(F32)).astype(BF16)
    mine = g0.astype(F32) + swap(g1, "tensor", 1).astype(F32)
    mine = (mine + swap(far, "tensor", 2).astype(F32)).astype(BF16)
    return sum_over_dp(mine).astype(F32)


def small_sum(values):
    for bit in (1, 2):
        values = values + swap(values, "tensor", bit)
    for bit in dp_bits():
        values = values + swap(values, "dp", bit)
    return values


def per_device(
    tokens,
    bucket,
    lengths,
    w_query,
    b_query,
    w_key,
    w_value,
    b_value,
    w_out,
    b_out,
    gain1,
    shift1,
    w_in,
    b_in,
    w_down,
    b_down,
    gain2,
    shift2,
    cotangent,
):
    rows = tokens.shape[0]
    width = w_query.shape[1]
    row_of, valid = row_layout(bucket, lengths, lax.axis_index("tensor") * rows, rows)
    biases = pieces_of(jnp.concatenate((b_query, b_value, b_in)))
    w_qkv = pieces_of(jnp.concatenate((w_query, w_key, w_value), axis=1))
    w_outs = pieces_of(w_out)
    w_ins = pieces_of(w_in)
    w_downs = pieces_of(w_down)

    q, k, v = [], [], []
    for weight, bias in zip(w_qkv, biases):
        joined = jnp.concatenate((bias[:width], jnp.zeros_like(bias[:width]), bias[width : 2 * width]))
        out = (product(tokens, weight) + joined.astype(F32)).astype(BF16)
        q.append(out[:, :width])
        k.append(out[:, width : 2 * width])
        v.append(out[:, 2 * width :])
    q, k, v = [jnp.concatenate(item, axis=1) for item in (q, k, v)]
    context, log_total = attend_forward(q, k, v, row_of, valid)
    attention = b_out.astype(F32)
    for at, weight in enumerate(w_outs):
        attention = attention + product(context[:, at * width : (at + 1) * width], weight)
    residual = tokens.astype(F32) + attention
    normed = norm_rows(residual, gain1, shift1)
    normed_low = normed.astype(BF16)
    pre, act = [], []
    ffn_out = b_down.astype(F32)
    for weight, down, bias in zip(w_ins, w_downs, biases):
        pre.append(product(normed_low, weight) + bias[2 * width :].astype(F32))
        act.append(exact_gelu(pre[-1]).astype(BF16))
        ffn_out = ffn_out + product(act[-1], down)
    summed = normed + ffn_out
    result, norm2_pull = jax.vjp(norm_rows, summed, gain2, shift2)
    grad_summed, grad_gain2, grad_shift2 = norm2_pull(cotangent)
    grad_ffn = grad_summed.astype(BF16)
    grad_bdown = jnp.sum(grad_ffn.astype(F32), axis=0)
    grad_downs = [rows_product(item, grad_ffn) for item in act]
    grad_ins, grad_bins = [], []
    grad_normed = grad_summed
    for at in range(4):
        grad_act = back_product(grad_ffn, w_downs[at])
        grad_pre = jax.vjp(exact_gelu, pre[at])[1](grad_act)[0].astype(BF16)
        grad_ins.append(rows_product(normed_low, grad_pre))
        grad_bins.append(jnp.sum(grad_pre.astype(F32), axis=0))
        grad_normed = grad_normed + back_product(grad_pre, w_ins[at])
    grad_resid, grad_gain1, grad_shift1 = jax.vjp(norm_rows, residual, gain1, shift1)[1](
        grad_normed
    )
    grad_attn = grad_resid.astype(BF16)
    grad_bout = jnp.sum(grad_attn.astype(F32), axis=0)
    grad_outs = [
        rows_product(context[:, at * width : (at + 1) * width], grad_attn) for at in range(4)
    ]
    grad_context = jnp.concatenate(
        [back_product(grad_attn, weight).astype(BF16) for weight in w_outs], axis=1
    )
    gq, gk, gv = attend_backward(q, k, v, grad_context, log_total, row_of, valid)
    grad_tokens = grad_resid
    grad_qkvs, grad_bq, grad_bv = [], [], []
    for at in range(4):
        cols = slice(at * width, (at + 1) * width)
        joined = jnp.concatenate((gq[:, cols], gk[:, cols], gv[:, cols]), axis=1)
        grad_qkvs.append(rows_product(tokens, joined))
        grad_tokens = grad_tokens + back_product(joined, w_qkv[at])
        sums = jnp.sum(joined.astype(F32), axis=0)
        grad_bq.append(sums[:width])
        grad_bv.append(sums[2 * width :])

    grad_wd = to_owner(grad_downs)
    grad_wi = to_owner(grad_ins)
    grad_wo = to_owner(grad_outs)
    grad_wqkv = to_owner(grad_qkvs)

    me = lax.axis_index("tensor")
    order = me ^ jnp.arange(4)
    split = jnp.stack(
        [jnp.concatenate((grad_bq[at], grad_bv[at], grad_bins[at])) for at in range(4)]
    )
    split = jnp.take(split, order, axis=0)
    small = jnp.stack((grad_bout, grad_gain1, grad_shift1, grad_bdown, grad_gain2, grad_shift2))
    flat = small_sum(jnp.concatenate((small.reshape(-1), split.reshape(-1))).reshape(-1, 128))
    flat = flat.reshape(-1)
    small = flat[: small.size].reshape(small.shape)
    split = lax.dynamic_index_in_dim(flat[small.size :].reshape(split.shape), me, 0, False)
    return (
        result.astype(BF16),
        grad_tokens,
        grad_wqkv[:, :width],
        split[:width],
        grad_wqkv[:, width : 2 * width],
        grad_wqkv[:, 2 * width :],
        split[width : 2 * width],
        grad_wo,
        small[0],
        small[1],
        small[2],
        grad_wi,
        split[2 * width :],
        grad_wd,
        small[3],
        small[4],
        small[5],
    )


def solution(mesh):
    group = P(("dp", "tensor"), None)
    column, row, part, whole = P(None, "tensor"), P("tensor", None), P("tensor"), P()
    in_specs = (
        group, P("dp"), P("dp", None), column, part, column, column, part, row,
        whole, whole, whole, column, part, row, whole, whole, whole, group,
    )
    out_specs = (
        group, group, column, part, column, column, part, row,
        whole, whole, whole, column, part, row, whole, whole, whole,
    )
    return jax.shard_map(
        per_device, mesh=mesh, in_specs=in_specs, out_specs=out_specs, check_vma=False
    )
```

time: 1130 us -> 527 us (0.47)
  waiting for transfers between devices: 685 us -> 119 us
  blocking collectives: 63.2 us -> 0 us
  starting transfers between devices: 1.01 us -> 55.9 us
  matrix products: 231 us -> 200 us
  local copies, waits for them, and re-layouts: 63.2 us -> 83 us
  between operations: 15.5 us -> 3.54 us
    reduce_scatter x4 -> x0, waiting for transfers between devices: 296 us -> none  [the longest x1 99.2 us: back_total(): return lax.psum_scatter(values, 'tensor', scatter_dimension=0, tiled=True)]
    psum x1 -> x0, waiting for transfers between devices: 204 us -> none  [per_device(): lax.psum((split_grads[0], split_grads[1], split_grads[2], split_grads[3],...]
    all_gather x4 -> x0, waiting for transfers between devices: 184 us -> none  [the longest x1 46.5 us: resid_wide(): return lax.all_gather(values, 'tensor', axis=0, tiled=True)]
    ppermute x0 -> x56, waiting for transfers between devices: none -> 119 us  [swap(): return lax.ppermute(values, axis, [(at, at ^ bit) for at in range(count)])]
    psum x2 -> x0, blocking collectives: 63.2 us -> none  [the longest x1 40.7 us: per_device(): lax.psum((small_grads[0], small_grads[1], small_grads[2], small_grads[3],...]
    ppermute x0 -> x56, starting transfers between devices: none -> 55.9 us  [swap(): return lax.ppermute(values, axis, [(at, at ^ bit) for at in range(count)])]
    dot_general x52 -> x28, matrix products: 146 us -> 121 us  [the longest x16 78.4 us: product(): return jnp.dot(left, right, preferred_element_type=F32)]
    convert_element_type x13 -> x30, other arithmetic: 9.09 us -> 30.4 us  [the longest x2 14.2 us: one_block(): grad_scores = (probs * (grad_probs - centre)).astype(BF16)]
  transfers between devices with their start and end apart: 9 -> 56, of which waited for: 8 -> 22; matrix products, arithmetic and copies ran while one was open for 4% -> 38% of each run, Pallas kernels for 0% -> 0%
where the time goes in v1:
time: 527 us; the launch traced here: 518 us
  matrix products  200 us (38%)
  waiting for transfers between devices  119 us (23%)
  local copies, waits for them, and re-layouts  83 us (16%)
  starting transfers between devices  55.9 us (11%)
  other arithmetic  55.6 us (11%)
    ppermute x56, waiting for transfers between devices, swap(): return lax.ppermute(values, axis, [(at, at ^ bit) for at in range(count)])  119 us
    dot_general x16, matrix products, product(): return jnp.dot(left, right, preferred_element_type=F32)  78.4 us
    ppermute x56, starting transfers between devices, swap(): return lax.ppermute(values, axis, [(at, at ^ bit) for at in range(count)])  55.9 us
    dot_general x16, matrix products, back_product(): lax.dot_general(left, right, (((1,), (1,)), ((), ())), preferred_element_...  45.5 us
    dot_general x16, matrix products, rows_product(): lax.dot_general(left, right, (((0,), (0,)), ((), ())), preferred_element_...  29.4 us
    unnamed x226, local copies, waits for them, and re-layouts  25.5 us
    convert_element_type x2, other arithmetic, one_block(): grad_scores = (probs * (grad_probs - centre)).astype(BF16)  14.2 us
    dot_general x2, matrix products, one_block(): jnp.einsum('qhd,khd->hqk', grad_blk, value_blk, preferred_element_type=F32)  13.7 us
  transfers between devices with their start and end apart: 56, of which 22 were waited for; matrix products, arithmetic and copies ran while one was open for 38% of the time, Pallas kernels for 0%

profile of v1, /device:TPU:0, one launch (start us, length us, event | category | flops | bytes accessed | tf_op | source)
XLA Modules:
  0.0 517.9 jit_solution(14009454012368319609)
XLA Ops:
  57.8 22.7 %while.26 = (s32[]{:T(128)}, bf16[2,512,12,64]{1,3,2,0:T(8,128)(2,1)}, f32[2,12,512]{2,1,0:T(8,128)}, bf16[2,512,12,64]{1,3,2,0:T(8,128)(2,1)}, s32[2,512]{1,0:T...) while((s32[]{:T(128)}, ...), condition=%wide.region_4.5_spmd, body=%wide.region_1.4_spmd.sunk | while | flops 843573248 | bytes 42944612 | solution.py:73
  63.8 5.5 %bitcast_dynamic-update-slice_fusion.10 = bf16[2,512,12,64]{1,3,2,0:T(8,128)(2,1)} fusion(bf16[2,512,12,64]{1,3,2,0:T(8,128)(2,1)} %get-tuple-element.502, s32[]{:T(128)} %get-tuple-element.501, f32[12,512,512]{1,2,0:T(8,128)S(1)} %get-tuple-element.477, f32[12,512]{1,0:T(8,128)S(1)} %fusion.239, f32[12,512]{1,0:T(8,128)S(1)} %get-tuple-element.478, ...), kind=kOutput, calls=%fused_computation.7.clone.1 | convolution fusion | flops 418381824 | bytes 15254528 | tf_op jit(solution)/shard_map/while/body/eval_jaxpr/hqk,khd->qhd/dot_general | solution.py:70
  74.9 5.5 %bitcast_dynamic-update-slice_fusion.10 = bf16[2,512,12,64]{1,3,2,0:T(8,128)(2,1)} fusion(bf16[2,512,12,64]{1,3,2,0:T(8,128)(2,1)} %get-tuple-element.502, s32[]{:T(128)} %get-tuple-element.501, f32[12,512,512]{1,2,0:T(8,128)S(1)} %get-tuple-element.477, f32[12,512]{1,0:T(8,128)S(1)} %fusion.239, f32[12,512]{1,0:T(8,128)S(1)} %get-tuple-element.478, ...), kind=kOutput, calls=%fused_computation.7.clone.1 | convolution fusion | flops 418381824 | bytes 15254528 | tf_op jit(solution)/shard_map/while/body/eval_jaxpr/hqk,khd->qhd/dot_general | solution.py:70
  95.4 11.4 %multiply_convert_fusion.4 = (bf16[1024,768]{1,0:T(8,128)(2,1)S(1)}, f32[1024,768]{1,0:T(8,128)}, f32[1024,768]{1,0:T(8,128)}) fusion(f32[768]{0:T(1024)S(1)} %copy-done.94, bf16[1024,768]{0,1:T(8,128)(2,1)S(1)} %fusion.67, bf16[768,768]{1,0:T(8,128)(2,1)} %param.35), kind=kOutput, calls=%fused_computation.127 | convolution fusion | flops 1259864064 | bytes 10619904 | tf_op jit(solution)/shard_map/dot_general | solution.py:25
  106.9 19.8 %multiply_convert_fusion.2 = (bf16[1024,768]{1,0:T(8,128)(2,1)S(1)}, f32[1024,768]{1,0:T(8,128)S(1)}, f32[1024,768]{1,0:T(8,128)S(1)}) fusion(f32[768]{0:T(1024)S(1)} %copy-done.96, bf16[1024,768]{0,1:T(8,128)(2,1)S(1)} %fusion.67, bf16[768,768]{1,0:T(8,128)(2,1)} %collective-permute-done.11), kind=kOutput, calls=%fused_computation.101 | convolution fusion | flops 1259864064 | bytes 10619904 | tf_op jit(solution)/shard_map/dot_general | solution.py:25
  126.7 11.9 %multiply_convert_fusion.3 = (bf16[1024,768]{1,0:T(8,128)(2,1)S(1)}, f32[1024,768]{1,0:T(8,128)}, f32[1024,768]{1,0:T(8,128)}) fusion(f32[768]{0:T(1024)S(1)} %copy-done.97, bf16[1024,768]{0,1:T(8,128)(2,1)S(1)} %fusion.67, bf16[768,768]{1,0:T(8,128)(2,1)} %collective-permute-done.9), kind=kOutput, calls=%fused_computation.114 | convolution fusion | flops 1259864064 | bytes 10619904 | tf_op jit(solution)/shard_map/dot_general | solution.py:25
  145.7 9.9 %multiply_convert_fusion.1 = (bf16[1024,768]{1,0:T(8,128)(2,1)S(1)}, f32[1024,768]{1,0:T(8,128)}, f32[1024,768]{1,0:T(8,128)}) fusion(f32[768]{0:T(1024)S(1)} %copy-done.98, bf16[1024,768]{0,1:T(8,128)(2,1)S(1)} %fusion.67, bf16[768,768]{1,0:T(8,128)(2,1)S(1)} %collective-permute-done.13), kind=kOutput, calls=%fused_computation.88 | convolution fusion | flops 1259864064 | bytes 10619904 | tf_op jit(solution)/shard_map/dot_general | solution.py:25
  181.2 4.5 convert_reduce_fusion.3
  192.4 4.5 convert_reduce_fusion.1
  200.6 4.4 convert_reduce_fusion
  226.6 49.1 %while.27 = (s32[]{:T(128)}, bf16[2,512,12,64]{1,3,2,0:T(8,128)(2,1)}, bf16[2,512,12,64]{1,3,2,0:T(8,128)(2,1)}, bf16[2,512,12,64]{1,3,2,0:T(8,128)(2,1)}, bf16[...) while((s32[]{:T(128)}, ...), condition=%wide.region_15.16_spmd, body=%wide.region_13.15_spmd.sunk | while | flops 2061756416 | bytes 149885776 | solution.py:105
  228.8 6.8 %multiply_reduce_fusion.8 = (f32[12,512]{1,0:T(8,128)S(1)}, f32[12,512,512]{1,2,0:T(8,128)}) fusion(f32[12,512,512]{1,2,0:T(8,128)S(1)} %fusion.248, f32[12,512]{1,0:T(8,128)S(1)} %dynamic-slice_bitcast_fusion.2, pred[512,512]{0,1:T(8,128)(4,1)S(1)} %compare_and_fusion.6, bf16[2,512,12,64]{1,3,2,0:T(8,128)(2,1)S(1)} %copy-done.11, ...), kind=kOutput, calls=%fused_computation.24.clone.1 | convolution fusion | flops 418375680 | bytes 27059200 | tf_op jit(solution)/shard_map/while/body/eval_jaxpr/qhd,khd->hqk/dot_general | solution.py:91
  235.6 7.1 %multiply_convert_fusion.6 = bf16[12,512,512]{1,2,0:T(8,128)(2,1)S(1)} fusion(f32[12,512,512]{1,2,0:T(8,128)} %get-tuple-element.490, f32[12,512,512]{1,2,0:T(8,128)S(1)} %fusion.248, f32[12,512]{1,0:T(8,128)S(1)} %get-tuple-element.491, f32[12,512]{1,0:T(8,128)S(1)} %dynamic-slice_bitcast_fusion.2, pred[512,512]{0,1:T(8,128)(4,1)S(1)} %compare_and_fusion.6), kind=kLoop, calls=%fused_computation.23.clone.1 | loop fusion | flops 18874368 | bytes 31768576 | tf_op jit(solution)/shard_map/while/body/eval_jaxpr/convert_element_type | solution.py:93
  253.2 6.8 %multiply_reduce_fusion.8 = (f32[12,512]{1,0:T(8,128)S(1)}, f32[12,512,512]{1,2,0:T(8,128)}) fusion(f32[12,512,512]{1,2,0:T(8,128)S(1)} %fusion.248, f32[12,512]{1,0:T(8,128)S(1)} %dynamic-slice_bitcast_fusion.2, pred[512,512]{0,1:T(8,128)(4,1)S(1)} %compare_and_fusion.6, bf16[2,512,12,64]{1,3,2,0:T(8,128)(2,1)S(1)} %copy-done.11, ...), kind=kOutput, calls=%fused_computation.24.clone.1 | convolution fusion | flops 418375680 | bytes 27059200 | tf_op jit(solution)/shard_map/while/body/eval_jaxpr/qhd,khd->hqk/dot_general | solution.py:91
  260.1 7.1 %multiply_convert_fusion.6 = bf16[12,512,512]{1,2,0:T(8,128)(2,1)S(1)} fusion(f32[12,512,512]{1,2,0:T(8,128)} %get-tuple-element.490, f32[12,512,512]{1,2,0:T(8,128)S(1)} %fusion.248, f32[12,512]{1,0:T(8,128)S(1)} %get-tuple-element.491, f32[12,512]{1,0:T(8,128)S(1)} %dynamic-slice_bitcast_fusion.2, pred[512,512]{0,1:T(8,128)(4,1)S(1)} %compare_and_fusion.6), kind=kLoop, calls=%fused_computation.23.clone.1 | loop fusion | flops 18874368 | bytes 31768576 | tf_op jit(solution)/shard_map/while/body/eval_jaxpr/convert_element_type | solution.py:93
  322.3 6.9 %collective-permute-done.31 = bf16[192,768]{1,0:T(8,128)(2,1)S(1)} collective-permute-done((bf16[192,768]{1,0:T(8,128)(2,1)S(1)}, bf16[192,768]{1,0:T(8,128)(2,1)S(1)}, u32[]{:S(2)}, u32[]{:S(2)}) %collective-permute-start.31) | collective-permute-done | bytes 294944 | tf_op jit(solution)/shard_map/ppermute | solution.py:122
  356.8 12.1 %collective-permute-done.17 = bf16[768,576]{0,1:T(8,128)(2,1)S(1)} collective-permute-done((bf16[768,576]{0,1:T(8,128)(2,1)S(1)}, bf16[768,576]{0,1:T(8,128)(2,1)S(1)}, u32[]{:S(2)}, u32[]{:S(2)}) %collective-permute-start.17) | collective-permute-done | bytes 884768 | tf_op jit(solution)/shard_map/ppermute | solution.py:122
  387.7 10.4 %collective-permute-done.49 = bf16[768,768]{1,0:T(8,128)(2,1)} collective-permute-done((bf16[768,768]{1,0:T(8,128)(2,1)}, bf16[768,768]{1,0:T(8,128)(2,1)}, u32[]{:S(2)}, u32[]{:S(2)}) %collective-permute-start.49) | collective-permute-done | bytes 1179680 | tf_op jit(solution)/shard_map/ppermute | solution.py:122
  401.8 19.8 %collective-permute-done.40 = bf16[768,768]{1,0:T(8,128)(2,1)} collective-permute-done((bf16[768,768]{1,0:T(8,128)(2,1)}, bf16[768,768]{1,0:T(8,128)(2,1)}, u32[]{:S(2)}, u32[]{:S(2)}) %collective-permute-start.40) | collective-permute-done | bytes 1179680 | tf_op jit(solution)/shard_map/ppermute | solution.py:122
  443.9 13.2 %collective-permute-done.51 = bf16[192,768]{1,0:T(8,128)(2,1)S(1)} collective-permute-done((bf16[192,768]{1,0:T(8,128)(2,1)S(1)}, bf16[192,768]{1,0:T(8,128)(2,1)S(1)}, u32[]{:S(2)}, u32[]{:S(2)}) %collective-permute-start.51) | collective-permute-done | bytes 294944 | tf_op jit(solution)/shard_map/ppermute | solution.py:122
  464.0 7.3 %collective-permute-done.52 = bf16[96,768]{1,0:T(8,128)(2,1)S(1)} collective-permute-done((bf16[96,768]{1,0:T(8,128)(2,1)S(1)}, bf16[96,768]{1,0:T(8,128)(2,1)S(1)}, u32[]{:S(2)}, u32[]{:S(2)}) %collective-permute-start.52) | collective-permute-done | bytes 147488 | tf_op jit(solution)/shard_map/ppermute | solution.py:122
  474.4 5.7 %collective-permute-done.53 = bf16[96,768]{1,0:T(8,128)(2,1)S(1)} collective-permute-done((bf16[96,768]{1,0:T(8,128)(2,1)S(1)}, bf16[96,768]{1,0:T(8,128)(2,1)S(1)}, u32[]{:S(2)}, u32[]{:S(2)}) %collective-permute-start.53) | collective-permute-done | bytes 147488 | tf_op jit(solution)/shard_map/ppermute | solution.py:122
  497.4 9.3 %collective-permute-done.55 = bf16[384,768]{1,0:T(8,128)(2,1)S(1)} collective-permute-done((bf16[384,768]{1,0:T(8,128)(2,1)S(1)}, bf16[384,768]{1,0:T(8,128)(2,1)S(1)}, u32[]{:S(2)}, u32[]{:S(2)}) %collective-permute-start.55) | collective-permute-done | bytes 589856 | tf_op jit(solution)/shard_map/ppermute | solution.py:122
  508.3 7.5 %collective-permute-done.46 = bf16[384,768]{1,0:T(8,128)(2,1)S(1)} collective-permute-done((bf16[384,768]{1,0:T(8,128)(2,1)S(1)}, bf16[384,768]{1,0:T(8,128)(2,1)S(1)}, u32[]{:S(2)}, u32[]{:S(2)}) %collective-permute-start.46) | collective-permute-done | bytes 589856 | tf_op jit(solution)/shard_map/ppermute | solution.py:122
  (573 shorter events, 315.9 us)
Async XLA Ops:
  11.1 22.8 %collective-permute-start.2 = (bf16[768,576]{0,1:T(8,128)(2,1)}, bf16[768,576]{0,1:T(8,128)(2,1)}, u32[]{:S(2)}, u32[]{:S(2)}) collective-permute-start(bf16[768,576]{0,1:T(8,128)(2,1)} %constant_dynamic-update-slice_fusion), channel_id=1, source_target_pairs={{0,2},{1,3},{2,0},{3,1},{4,6},{5,7},{6,4},{7,5},{8,10},{9,11},{10,... | collective-permute-start | bytes 2654216 | tf_op jit(solution)/shard_map/ppermute | solution.py:122
  11.2 25.9 %collective-permute-start = (bf16[768,576]{0,1:T(8,128)(2,1)}, bf16[768,576]{0,1:T(8,128)(2,1)}, u32[]{:S(2)}, u32[]{:S(2)}) collective-permute-start(bf16[768,576]{0,1:T(8,128)(2,1)} %constant_dynamic-update-slice_fusion), channel_id=1, source_target_pairs={{0,1},{1,0},{2,3},{3,2},{4,5},{5,4},{6,7},{7,6},{8,9},{9,8},{10,11... | collective-permute-start | bytes 2654216 | tf_op jit(solution)/shard_map/ppermute | solution.py:122
  11.6 77.1 %collective-permute-start.6 = (bf16[192,768]{1,0:T(8,128)(2,1)}, bf16[192,768]{1,0:T(8,128)(2,1)}, u32[]{:S(2)}, u32[]{:S(2)}) collective-permute-start(bf16[192,768]{1,0:T(8,128)(2,1)} %param.31), channel_id=1, source_target_pairs={{0,1},{1,0},{2,3},{3,2},{4,5},{5,4},{6,7},{7,6},{8,9},{9,8},{10,11... | collective-permute-start | bytes 884744 | tf_op jit(solution)/shard_map/ppermute | solution.py:122
  22.7 64.3 %collective-permute-start.7 = (bf16[192,768]{1,0:T(8,128)(2,1)}, bf16[192,768]{1,0:T(8,128)(2,1)}, u32[]{:S(2)}, u32[]{:S(2)}) collective-permute-start(bf16[192,768]{1,0:T(8,128)(2,1)} %param.31), channel_id=1, source_target_pairs={{0,2},{1,3},{2,0},{3,1},{4,6},{5,7},{6,4},{7,5},{8,10},{9,11},{10,... | collective-permute-start | bytes 884744 | tf_op jit(solution)/shard_map/ppermute | solution.py:122
  26.5 100.1 %collective-permute-start.9 = (bf16[768,768]{1,0:T(8,128)(2,1)}, bf16[768,768]{1,0:T(8,128)(2,1)}, u32[]{:S(2)}, u32[]{:S(2)}) collective-permute-start(bf16[768,768]{1,0:T(8,128)(2,1)} %param.35), channel_id=1, source_target_pairs={{0,1},{1,0},{2,3},{3,2},{4,5},{5,4},{6,7},{7,6},{8,9},{9,8},{10,11... | collective-permute-start | bytes 3538952 | tf_op jit(solution)/shard_map/ppermute | solution.py:122
  37.0 52.2 %collective-permute-start.11 = (bf16[768,768]{1,0:T(8,128)(2,1)}, bf16[768,768]{1,0:T(8,128)(2,1)}, u32[]{:S(2)}, u32[]{:S(2)}) collective-permute-start(bf16[768,768]{1,0:T(8,128)(2,1)} %param.35), channel_id=1, source_target_pairs={{0,2},{1,3},{2,0},{3,1},{4,6},{5,7},{6,4},{7,5},{8,10},{9,11},{10,... | collective-permute-start | bytes 3538952 | tf_op jit(solution)/shard_map/ppermute | solution.py:122
  40.2 50.8 %collective-permute-start.12 = (bf16[768,768]{1,0:T(8,128)(2,1)}, bf16[768,768]{1,0:T(8,128)(2,1)}, u32[]{:S(2)}, u32[]{:S(2)}) collective-permute-start(bf16[768,768]{1,0:T(8,128)(2,1)} %param.37), channel_id=1, source_target_pairs={{0,2},{1,3},{2,0},{3,1},{4,6},{5,7},{6,4},{7,5},{8,10},{9,11},{10,... | collective-permute-start | bytes 3538952 | tf_op jit(solution)/shard_map/ppermute | solution.py:122
  87.0 57.1 %collective-permute-start.10 = (bf16[768,768]{1,0:T(8,128)(2,1)}, bf16[768,768]{1,0:T(8,128)(2,1)S(1)}, u32[]{:S(2)}, u32[]{:S(2)}) collective-permute-start(bf16[768,768]{1,0:T(8,128)(2,1)} %param.37), channel_id=1, source_target_pairs={{0,1},{1,0},{2,3},{3,2},{4,5},{5,4},{6,7},{7,6},{8,9},{9,8},{10,11... | collective-permute-start | bytes 3538952 | tf_op jit(solution)/shard_map/ppermute | solution.py:122
  89.2 56.5 %collective-permute-start.13 = (bf16[768,768]{1,0:T(8,128)(2,1)}, bf16[768,768]{1,0:T(8,128)(2,1)S(1)}, u32[]{:S(2)}, u32[]{:S(2)}) collective-permute-start(bf16[768,768]{1,0:T(8,128)(2,1)} %collective-permute-done.11), channel_id=1, source_target_pairs={{0,1},{1,0},{2,3},{3,2},{4,5},{5,4},{6,7},{7,6},{8,9},{9,8},{10,11... | collective-permute-start | bytes 3538952 | tf_op jit(solution)/shard_map/ppermute | solution.py:122
  91.0 64.6 %collective-permute-start.14 = (bf16[768,768]{1,0:T(8,128)(2,1)}, bf16[768,768]{1,0:T(8,128)(2,1)}, u32[]{:S(2)}, u32[]{:S(2)}) collective-permute-start(bf16[768,768]{1,0:T(8,128)(2,1)} %collective-permute-done.12), channel_id=1, source_target_pairs={{0,1},{1,0},{2,3},{3,2},{4,5},{5,4},{6,7},{7,6},{8,9},{9,8},{10,11... | collective-permute-start | bytes 3538952 | tf_op jit(solution)/shard_map/ppermute | solution.py:122
  291.4 55.8 %collective-permute-start.48 = (bf16[768,768]{1,0:T(8,128)(2,1)}, bf16[768,768]{1,0:T(8,128)(2,1)}, u32[]{:S(2)}, u32[]{:S(2)}) collective-permute-start(bf16[768,768]{1,0:T(8,128)(2,1)} %convolution_convert_fusion), channel_id=1, source_target_pairs={{0,1},{1,0},{2,3},{3,2},{4,5},{5,4},{6,7},{7,6},{8,9},{9,8},{10,11... | collective-permute-start | bytes 3538952 | tf_op jit(solution)/shard_map/ppermute | solution.py:122
  291.9 25.0 %collective-permute-start.30 = (bf16[192,768]{1,0:T(8,128)(2,1)}, bf16[192,768]{1,0:T(8,128)(2,1)}, u32[]{:S(2)}, u32[]{:S(2)}) collective-permute-start(bf16[192,768]{1,0:T(8,128)(2,1)} %convolution_convert_fusion.16), channel_id=1, source_target_pairs={{0,1},{1,0},{2,3},{3,2},{4,5},{5,4},{6,7},{7,6},{8,9},{9,8},{10,11... | collective-permute-start | bytes 884744 | tf_op jit(solution)/shard_map/ppermute | solution.py:122
  292.0 30.3 %collective-permute-start.29 = (bf16[192,768]{1,0:T(8,128)(2,1)}, bf16[192,768]{1,0:T(8,128)(2,1)}, u32[]{:S(2)}, u32[]{:S(2)}) collective-permute-start(bf16[192,768]{1,0:T(8,128)(2,1)} %convolution_convert_fusion.18), channel_id=1, source_target_pairs={{0,1},{1,0},{2,3},{3,2},{4,5},{5,4},{6,7},{7,6},{8,9},{9,8},{10,11... | collective-permute-start | bytes 884744 | tf_op jit(solution)/shard_map/ppermute | solution.py:122
  344.3 42.8 %collective-permute-start.47 = (bf16[768,768]{1,0:T(8,128)(2,1)}, bf16[768,768]{1,0:T(8,128)(2,1)}, u32[]{:S(2)}, u32[]{:S(2)}) collective-permute-start(bf16[768,768]{1,0:T(8,128)(2,1)} %convolution_convert_fusion.2), channel_id=1, source_target_pairs={{0,1},{1,0},{2,3},{3,2},{4,5},{5,4},{6,7},{7,6},{8,9},{9,8},{10,11... | collective-permute-start | bytes 3538952 | tf_op jit(solution)/shard_map/ppermute | solution.py:122
  345.5 56.3 %collective-permute-start.38 = (bf16[768,768]{1,0:T(8,128)(2,1)}, bf16[768,768]{1,0:T(8,128)(2,1)}, u32[]{:S(2)}, u32[]{:S(2)}) collective-permute-start(bf16[768,768]{1,0:T(8,128)(2,1)} %convolution_convert_fusion.6), channel_id=1, source_target_pairs={{0,1},{1,0},{2,3},{3,2},{4,5},{5,4},{6,7},{7,6},{8,9},{9,8},{10,11... | collective-permute-start | bytes 3538952 | tf_op jit(solution)/shard_map/ppermute | solution.py:122
  347.2 21.7 %collective-permute-start.17 = (bf16[768,576]{0,1:T(8,128)(2,1)S(1)}, bf16[768,576]{0,1:T(8,128)(2,1)S(1)}, u32[]{:S(2)}, u32[]{:S(2)}) collective-permute-start(bf16[768,576]{0,1:T(8,128)(2,1)S(1)} %fusion.68), channel_id=1, source_target_pairs={{0,2},{1,3},{2,0},{3,1},{4,6},{5,7},{6,4},{7,5},{8,10},{9,11},{10,... | collective-permute-start | bytes 2654216 | tf_op jit(solution)/shard_map/ppermute | solution.py:122
  368.9 29.2 %collective-permute-start.49 = (bf16[768,768]{1,0:T(8,128)(2,1)}, bf16[768,768]{1,0:T(8,128)(2,1)}, u32[]{:S(2)}, u32[]{:S(2)}) collective-permute-start(bf16[768,768]{1,0:T(8,128)(2,1)} %add_convert_fusion.8), channel_id=1, source_target_pairs={{0,2},{1,3},{2,0},{3,1},{4,6},{5,7},{6,4},{7,5},{8,10},{9,11},{10,... | collective-permute-start | bytes 3538952 | tf_op jit(solution)/shard_map/ppermute | solution.py:122
  371.6 50.0 %collective-permute-start.40 = (bf16[768,768]{1,0:T(8,128)(2,1)}, bf16[768,768]{1,0:T(8,128)(2,1)}, u32[]{:S(2)}, u32[]{:S(2)}) collective-permute-start(bf16[768,768]{1,0:T(8,128)(2,1)} %add_convert_fusion.10), channel_id=1, source_target_pairs={{0,2},{1,3},{2,0},{3,1},{4,6},{5,7},{6,4},{7,5},{8,10},{9,11},{10,... | collective-permute-start | bytes 3538952 | tf_op jit(solution)/shard_map/ppermute | solution.py:122
  384.3 48.7 %collective-permute-start.36 = (bf16[48,768]{1,0:T(8,128)(2,1)S(1)}, bf16[48,768]{1,0:T(8,128)(2,1)S(1)}, u32[]{:S(2)}, u32[]{:S(2)}) collective-permute-start(bf16[48,768]{1,0:T(8,128)(2,1)S(1)} %maximum_select_fusion.11), channel_id=1, source_target_pairs={{0,8},{4,12},{8,0},{12,4},{16,24},{20,28},{24,16},{28,20},{1,9},{5... | collective-permute-start | bytes 221192 | tf_op jit(solution)/shard_map/ppermute | solution.py:122
  387.1 36.5 %collective-permute-start.19 = (bf16[192,576]{0,1:T(8,128)(2,1)S(1)}, bf16[192,576]{0,1:T(8,128)(2,1)S(1)}, u32[]{:S(2)}, u32[]{:S(2)}) collective-permute-start(bf16[192,576]{0,1:T(8,128)(2,1)S(1)} %constant_dynamic-slice_fusion.13), channel_id=1, source_target_pairs={{0,8},{4,12},{8,0},{12,4},{16,24},{20,28},{24,16},{28,20},{1,9},{5... | collective-permute-start | bytes 663560 | tf_op jit(solution)/shard_map/ppermute | solution.py:122
  400.2 41.2 %collective-permute-start.50 = (bf16[384,768]{1,0:T(8,128)(2,1)S(1)}, bf16[384,768]{1,0:T(8,128)(2,1)S(1)}, u32[]{:S(2)}, u32[]{:S(2)}) collective-permute-start(bf16[384,768]{1,0:T(8,128)(2,1)S(1)} %constant_dynamic-slice_fusion.5), channel_id=1, source_target_pairs={{0,4},{4,0},{8,12},{12,8},{16,20},{20,16},{24,28},{28,24},{1,5},{5... | collective-permute-start | bytes 1769480 | tf_op jit(solution)/shard_map/ppermute | solution.py:122
  433.0 59.0 %collective-permute-start.37 = (bf16[96,768]{1,0:T(8,128)(2,1)S(1)}, bf16[96,768]{1,0:T(8,128)(2,1)S(1)}, u32[]{:S(2)}, u32[]{:S(2)}) collective-permute-start(bf16[96,768]{1,0:T(8,128)(2,1)S(1)} %maximum_select_fusion.10), channel_id=1, source_target_pairs={{0,4},{4,0},{8,12},{12,8},{16,20},{20,16},{24,28},{28,24},{1,5},{5... | collective-permute-start | bytes 442376 | tf_op jit(solution)/shard_map/ppermute | solution.py:122
  438.9 43.0 %collective-permute-start.22 = (bf16[192,576]{0,1:T(8,128)(2,1)S(1)}, bf16[192,576]{0,1:T(8,128)(2,1)S(1)}, u32[]{:S(2)}, u32[]{:S(2)}) collective-permute-start(bf16[192,576]{0,1:T(8,128)(2,1)S(1)} %maximum_select_fusion.6), channel_id=1, source_target_pairs={{0,8},{4,12},{8,0},{12,4},{16,24},{20,28},{24,16},{28,20},{1,9},{5... | collective-permute-start | bytes 663560 | tf_op jit(solution)/shard_map/ppermute | solution.py:122
  494.4 21.5 %collective-permute-start.46 = (bf16[384,768]{1,0:T(8,128)(2,1)S(1)}, bf16[384,768]{1,0:T(8,128)(2,1)S(1)}, u32[]{:S(2)}, u32[]{:S(2)}) collective-permute-start(bf16[384,768]{1,0:T(8,128)(2,1)S(1)} %maximum_select_fusion.3), channel_id=1, source_target_pairs={{0,4},{4,0},{8,12},{12,8},{16,20},{20,16},{24,28},{28,24},{1,5},{5... | collective-permute-start | bytes 1769480 | tf_op jit(solution)/shard_map/ppermute | solution.py:122
  (154 other events, 1244.2 us)
